TPU v7x, 512 devices: a whole 4x4x16 slice. The times are simulated.
512 devices in a mesh: lon: 64 (over z, y_hi, core), lat: 8 (over y_lo, x).
Axes of the slice: x: 4, y: 4 (y_hi: 2, y_lo: 2; y = y_hi * 2 + y_lo), z: 16, core: 2. Of those that a mesh axis runs over, the one named last changes fastest.
Arguments:
- patches: bfloat16 [768, 96, 2, 512], P('lon', 'lat'), may hold values from -6 to 6
- qkv_first: bfloat16 [512, 1536], P(None, 'lon'), may hold values from -2 to 2
- proj_first: bfloat16 [512, 512], P(None, 'lon'), may hold values from -1 to 1
- qkv_second: bfloat16 [512, 1536], P(None, 'lon'), may hold values from -2 to 2
- proj_second: bfloat16 [512, 512], P(None, 'lon'), may hold values from -1 to 1
- merge_weight: bfloat16 [2048, 1024], P(None, 'lon'), may hold values from -0.125 to 0.125
Outputs:
- merged: bfloat16 [384, 48, 2, 1024], P('lon', 'lat')
All inputs are finite; a program needn't handle non-finite values.
Results may differ from a plain program's by a relative error of at most 0.019.
Values may be sent and summed in bfloat16 or wider, within the bound.
A program may use at most 64 MiB of HBM per device.

v0:
```python
import jax
import jax.numpy as jnp
from jax import lax
from jax.sharding import PartitionSpec as P

HEADS = 16
WLON = 12
WLAT = 6
WLEV = 2


norm_epsilon = 1e-05
masked_score = -1e30


def from_behind(value, axis, steps):
    count = lax.axis_size(axis)
    pairs = [(source, (source + steps) % count) for source in range(count)]
    return lax.ppermute(value, axis, pairs)


def normalize(values):
    values = values.astype(jnp.float32)
    centred = values - jnp.mean(values, axis=-1, keepdims=True)
    variance = jnp.mean(centred * centred, axis=-1, keepdims=True)
    return (centred * lax.rsqrt(variance + norm_epsilon)).astype(jnp.bfloat16)


def region_labels(position, count, window, offset):
    return jnp.where(
        position < count - window, 0, jnp.where(position < count - offset, 1, 2)
    ).astype(jnp.int32)


def to_windows(grid):
    size_a, size_b, size_c, features = grid.shape
    grid = grid.reshape(size_a // WLON, WLON, size_b // WLAT, WLAT, size_c // WLEV, WLEV, features)
    grid = grid.transpose(0, 2, 4, 1, 3, 5, 6)
    return grid.reshape(-1, WLON * WLAT * WLEV, features)


def from_windows(flat_windows, size_a, size_b, size_c):
    features = flat_windows.shape[-1]
    grid = flat_windows.reshape(
        size_a // WLON, size_b // WLAT, size_c // WLEV, WLON, WLAT, WLEV, features
    )
    return grid.transpose(0, 3, 1, 4, 2, 5, 6).reshape(size_a, size_b, size_c, features)


def project(activations, shard, residual):
    complete = lax.all_gather(shard, "lon", axis=1, tiled=True)
    product = jnp.dot(activations, complete, preferred_element_type=jnp.float32)
    if residual is not None:
        product = product + residual.astype(jnp.float32)
    return product.astype(jnp.bfloat16)


def attend(packed, labels):
    token_count = packed.shape[0]
    width = packed.shape[1] // 3
    head_size = width // HEADS
    heads_view = packed.reshape(token_count, 3, HEADS, head_size)
    scores = jnp.einsum(
        "qhd,khd->hqk", heads_view[:, 0], heads_view[:, 1], preferred_element_type=jnp.float32
    )
    scores = scores * head_size ** (-0.5)
    same = labels[:, None] == labels[None, :]
    scores = jnp.where(same[None], scores, masked_score)
    highest = jnp.max(scores, axis=-1, keepdims=True)
    weights = jnp.exp(scores - highest)
    probs = (weights / jnp.sum(weights, axis=-1, keepdims=True)).astype(jnp.bfloat16)
    attended = jnp.einsum(
        "hqk,khd->qhd", probs, heads_view[:, 2], preferred_element_type=jnp.float32
    )
    return attended.reshape(token_count, width).astype(jnp.bfloat16)


def mix(packed_grid, labels_grid):
    size_a, size_b, size_c, features = packed_grid.shape
    windows = to_windows(packed_grid)
    marks = to_windows(labels_grid[..., None])[..., 0]
    result = lax.map(lambda couple: attend(couple[0], couple[1]), (windows, marks))
    return from_windows(result, size_a, size_b, size_c)


def qkv_grid(grid, w_qkv):
    width = grid.shape[-1]
    packed = project(normalize(grid.reshape(-1, width)), w_qkv, None)
    return packed.reshape(grid.shape[:3] + (3 * width,))


def first_block(stream, w_qkv, w_out):
    size_a, size_b, size_c, width = stream.shape
    flat_rows = stream.reshape(-1, width)
    packed = qkv_grid(stream, w_qkv)
    labels = jnp.zeros((size_a, size_b, size_c), jnp.int32)
    attended = mix(packed, labels)
    return project(attended.reshape(-1, width), w_out, flat_rows).reshape(stream.shape)


def second_block(stream, w_qkv, w_out):
    size_a, size_b, size_c, width = stream.shape
    lon_shift = WLON // 2
    lat_shift = WLAT // 2
    lev_shift = WLEV // 2
    lat_total = size_b * lax.axis_size("lat")
    lev_labels = region_labels(jnp.arange(size_c), size_c, WLEV, lev_shift)
    rolled = jnp.roll(stream, -lev_shift, 2)
    edge_strip = from_behind(rolled[:lon_shift], "lon", -1)
    rolled = jnp.concatenate([rolled[lon_shift:], edge_strip], axis=0)
    edge_strip = from_behind(rolled[:, :lat_shift], "lat", -1)
    rolled = jnp.concatenate([rolled[:, lat_shift:], edge_strip], axis=1)
    lat_rows = lax.axis_index("lat") * size_b + jnp.arange(size_b)
    lat_labels = region_labels(lat_rows, lat_total, WLAT, lat_shift)
    labels = jnp.broadcast_to(
        (lat_labels[:, None] * 3 + lev_labels[None, :])[None], rolled.shape[:3]
    )
    packed = qkv_grid(rolled, w_qkv)
    attended = mix(packed, labels)
    edge_strip = from_behind(attended[:, size_b - lat_shift :], "lat", 1)
    attended = jnp.concatenate([edge_strip, attended[:, : size_b - lat_shift]], axis=1)
    edge_strip = from_behind(attended[size_a - lon_shift :], "lon", 1)
    attended = jnp.concatenate([edge_strip, attended[: size_a - lon_shift]], axis=0)
    attended = jnp.roll(attended, lev_shift, 2)
    return project(attended.reshape(-1, width), w_out, stream.reshape(-1, width)).reshape(
        stream.shape
    )


def patch_merge(stream, shard):
    size_a, size_b, size_c, width = stream.shape
    quads = stream.reshape(size_a // 2, 2, size_b // 2, 2, size_c, width)
    quads = quads.transpose(0, 2, 4, 3, 1, 5).reshape(-1, 4 * width)
    result = project(normalize(quads), shard, None)
    return result.reshape(size_a // 2, size_b // 2, size_c, 2 * width)


def body(patches, qkv_first, proj_first, qkv_second, proj_second, merge_weight):
    first = first_block(patches, qkv_first, proj_first)
    second = second_block(first, qkv_second, proj_second)
    return patch_merge(second, merge_weight)


def solution(mesh):
    placed = (
        P("lon", "lat", None, None),
        P(None, "lon"),
        P(None, "lon"),
        P(None, "lon"),
        P(None, "lon"),
        P(None, "lon"),
    )
    return jax.shard_map(
        body, mesh=mesh, in_specs=placed, out_specs=P("lon", "lat", None, None), check_vma=False
    )
```

profile of v0, /device:TPU:1, one launch (start us, length us, event | category | flops | bytes accessed | tf_op | source)
XLA Modules:
  0.0 458.0 jit_solution(11245195616321391120)
XLA Ops:
  6.5 0.7 all-gather.4.cloned.1.call-update
  8.7 1.0 reshape.242
  9.8 1.3 convert_reduce_fusion
  11.1 1.6 multiply_reduce_fusion.3
  13.0 91.4 %all_gather.16 = bf16[512,512]{0,1:T(8,128)(2,1)} all-gather(bf16[512,8]{0,1:T(8,128)(2,1)S(1)} %copy-done.1), channel_id=1, replica_groups=mesh['lon'=64,'lat'=8] {'lon'}, dimensions={1}, use_global_device_ids=true | all-gather | bytes 532480 | tf_op jit(solution)/shard_map/all_gather | solution.py:51
  104.3 54.1 %all-gather.4.cloned.1.call-done = bf16[512,1536]{0,1:T(8,128)(2,1)} async-done(((bf16[512,24]{0,1:T(8,128)(2,1)}), bf16[512,1536]{0,1:T(8,128)(2,1)}) %all-gather.4.cloned.1.call-update) | async-done | bytes 1572880 | tf_op jit(solution)/shard_map/all_gather | solution.py:51
  158.4 2.1 convolution_convert_fusion.3
  160.9 0.7 copy.13
  161.6 1.0 copy.14
  162.7 6.4 %while.20 = (s32[]{:T(128)}, bf16[2,144,512]{1,2,0:T(8,128)(2,1)S(1)}, bf16[2,144,1536]{1,2,0:T(8,128)(2,1)S(1)}, s32[]{:T(128)}) while((s32[]{:T(128)}, bf16[2,144,512]{1,2,0:T(8,128)(2,1)S(1)}, bf16[2,144,1536]{1,2,0:T(8,128)(2,1)S(1)}, s32[]{:T(128)}) %tuple.42), condition=%wide.region_5.6_spmd, body=%wide.region_2.5_spmd.sunk | while | flops 44531856 | bytes 8709181 | solution.py:82
  163.3 2.3 fusion.46
  166.5 2.3 fusion.46
  171.7 2.1 collective-permute-start
  174.1 5.6 %collective-permute-done = bf16[6,12,2,512]{3,2,1,0:T(2,128)(2,1)S(1)} collective-permute-done((bf16[6,12,2,512]{3,2,1,0:T(2,128)(2,1)S(1)}, bf16[6,12,2,512]{3,2,1,0:T(2,128)(2,1)S(1)}, u32[]{:S(2)}, u32[]{:S(2)}) %collective-permute-start) | collective-permute-done | bytes 147488 | tf_op jit(solution)/shard_map/ppermute | solution.py:19
  179.8 4.5 collective-permute-start.1
  184.6 1.6 collective-permute-done.1
  188.2 109.9 %all-gather.6.cloned.1.call-done = bf16[512,1536]{0,1:T(8,128)(2,1)} async-done(((bf16[512,24]{0,1:T(8,128)(2,1)}), bf16[512,1536]{0,1:T(8,128)(2,1)}) %all-gather.6.cloned.1.call-update) | async-done | bytes 1572880 | tf_op jit(solution)/shard_map/all_gather | solution.py:51
  298.1 2.1 convolution_convert_fusion.2
  300.5 0.7 copy.17
  301.3 1.0 copy.18
  302.4 9.3 %while.21 = (s32[]{:T(128)}, bf16[2,144,512]{1,2,0:T(8,128)(2,1)S(1)}, bf16[2,144,1536]{1,2,0:T(8,128)(2,1)S(1)}, s32[2,144]{1,0:T(2,128)S(1)}, s32[]{:T(128)}) while((s32[]{:T(128)}, bf16[2,144,512]{1,2,0:T(8,128)(2,1)S(1)}, bf16[2,144,1536]{1,2,0:T(8,128)(2,1)S(1)}, s32[2,144]{1,0:T(2,128)S(1)}, s32[]{:T(128)}) %tuple.45), condition=%wide.region_11.12_spmd, body=%wide.region_8.11_spmd.sunk | while | flops 44552592 | bytes 5082121 | solution.py:82
  302.5 2.4 fusion.47
  305.0 2.0 convolution_convert_fusion.8
  307.2 2.4 fusion.47
  309.6 2.0 convolution_convert_fusion.8
  312.4 3.1 collective-permute-start.2
  315.7 4.4 collective-permute-done.2
  320.2 3.5 collective-permute-start.3
  323.7 74.8 %all_gather.18 = bf16[512,512]{0,1:T(8,128)(2,1)S(1)} all-gather(bf16[512,8]{0,1:T(8,128)(2,1)S(1)} %copy-done.2), channel_id=1, replica_groups=mesh['lon'=64,'lat'=8] {'lon'}, dimensions={1}, use_global_device_ids=true | all-gather | bytes 532480 | tf_op jit(solution)/shard_map/all_gather | solution.py:51
  403.3 43.9 %all-gather.8.cloned.1.call-done = bf16[2048,1024]{0,1:T(8,128)(2,1)} async-done(((bf16[2048,16]{0,1:T(8,128)(2,1)}), bf16[2048,1024]{0,1:T(8,128)(2,1)}) %all-gather.8.cloned.1.call-update) | async-done | bytes 4194320 | tf_op jit(solution)/shard_map/all_gather | solution.py:51
  447.2 3.6 convolution_convert_fusion.4
  450.8 0.7 reshape.241
  (77 shorter events, 15.7 us)
Async XLA Ops:
  6.5 6.4 %copy-start.1 = (bf16[512,8]{0,1:T(8,128)(2,1)S(1)}, bf16[512,8]{0,1:T(8,128)(2,1)}, u32[]{:S(2)}) copy-start(bf16[512,8]{0,1:T(8,128)(2,1)} %param.12) | copy-start | bytes 24580
  6.5 151.9 %all-gather.4.cloned.1.call-start = ((), (), s32[]{:S(2)}) async-start(), calls=%async_computation | async-start | bytes 1597440 | tf_op jit(solution)/shard_map/all_gather | solution.py:51
  7.3 290.9 %all-gather.6.cloned.1.call-start = ((), (), s32[]{:S(2)}) async-start(), calls=%async_computation.1 | async-start | bytes 1597440 | tf_op jit(solution)/shard_map/all_gather | solution.py:51
  8.0 439.2 %all-gather.8.cloned.1.call-start = ((), (), s32[]{:S(2)}) async-start(), calls=%async_computation.2 | async-start | bytes 4259840 | tf_op jit(solution)/shard_map/all_gather | solution.py:51
  169.1 1.0 copy-start
  171.7 8.0 %collective-permute-start = (bf16[6,12,2,512]{3,2,1,0:T(2,128)(2,1)S(1)}, bf16[6,12,2,512]{3,2,1,0:T(2,128)(2,1)S(1)}, u32[]{:S(2)}, u32[]{:S(2)}) collective-permute-start(bf16[6,12,2,512]{3,2,1,0:T(2,128)(2,1)S(1)} %get-tuple-element.72), channel_id=1, source_target_pairs={{0,504},{8,0},{16,8},{24,16},{32,24},{40,32},{48,40},{56,48},{64,5... | collective-permute-start | bytes 442376 | tf_op jit(solution)/shard_map/ppermute | solution.py:19
  179.8 6.4 %collective-permute-start.1 = (bf16[12,3,2,512]{3,2,1,0:T(2,128)(2,1)S(1)}, bf16[12,3,2,512]{3,2,1,0:T(2,128)(2,1)S(1)}, u32[]{:S(2)}, u32[]{:S(2)}) collective-permute-start(bf16[12,3,2,512]{3,2,1,0:T(2,128)(2,1)S(1)} %pad_maximum_fusion.3), channel_id=1, source_target_pairs={{0,7},{1,0},{2,1},{3,2},{4,3},{5,4},{6,5},{7,6},{8,15},{9,8},{10,9... | collective-permute-start | bytes 221192 | tf_op jit(solution)/shard_map/ppermute | solution.py:19
  311.6 12.1 %copy-start.2 = (bf16[512,8]{0,1:T(8,128)(2,1)S(1)}, bf16[512,8]{0,1:T(8,128)(2,1)}, u32[]{:S(2)}) copy-start(bf16[512,8]{0,1:T(8,128)(2,1)} %param.14) | copy-start | bytes 24580
  312.4 7.6 %collective-permute-start.2 = (bf16[12,3,2,512]{3,2,1,0:T(2,128)(2,1)S(1)}, bf16[12,3,2,512]{3,2,1,0:T(2,128)(2,1)S(1)}, u32[]{:S(2)}, u32[]{:S(2)}) collective-permute-start(bf16[12,3,2,512]{3,2,1,0:T(2,128)(2,1)S(1)} %slice.82), channel_id=1, source_target_pairs={{0,1},{1,2},{2,3},{3,4},{4,5},{5,6},{6,7},{7,0},{8,9},{9,10},{10,1... | collective-permute-start | bytes 221192 | tf_op jit(solution)/shard_map/ppermute | solution.py:19
  320.2 78.2 %collective-permute-start.3 = (bf16[6,12,2,512]{3,2,1,0:T(2,128)(2,1)S(1)}, bf16[6,12,2,512]{3,2,1,0:T(2,128)(2,1)S(1)}, u32[]{:S(2)}, u32[]{:S(2)}) collective-permute-start(bf16[6,12,2,512]{3,2,1,0:T(2,128)(2,1)S(1)} %fusion.26), channel_id=1, source_target_pairs={{0,8},{8,16},{16,24},{24,32},{32,40},{40,48},{48,56},{56,64},{64,7... | collective-permute-start | bytes 442376 | tf_op jit(solution)/shard_map/ppermute | solution.py:19
Sparse Core Ops, SparseCore 0:
  10.6 147.7 all-gather.3
  161.7 136.3 all-gather.5
  301.4 145.7 all-gather.7
where the time goes:
time: 459 us; the launch traced here: 458 us
  waiting for transfers between devices  222 us (48%)
  blocking collectives  166 us (36%)
  matrix products  18.9 us (4%)
  between operations  13.5 us (3%)
  starting transfers between devices  13.3 us (3%)
  other arithmetic  12.6 us (3%)
  local copies, waits for them, and re-layouts  12 us (3%)
    all_gather x3, waiting for transfers between devices, project(): complete = lax.all_gather(shard, 'lon', axis=1, tiled=True)  208 us
    all_gather x2, blocking collectives, project(): complete = lax.all_gather(shard, 'lon', axis=1, tiled=True)  166 us
    ppermute x4, starting transfers between devices, from_behind(): return lax.ppermute(value, axis, pairs)  13.2 us
    ppermute x4, waiting for transfers between devices, from_behind(): return lax.ppermute(value, axis, pairs)  11.5 us
  transfers between devices with their start and end apart: 7, of which 6 were waited for; matrix products, arithmetic and copies ran while one was open for 8% of the time, Pallas kernels for 0%

commit v1 on v0

v1 whole, which is shorter than its diff:
```python
import functools

import jax
import jax.numpy as jnp
import numpy as np
from jax import lax
from jax.experimental import pallas as pl
from jax.experimental.pallas import tpu as pltpu
from jax.sharding import PartitionSpec as P

D = 512
HEADS = 16
Z = 16
H = Z // 2
Q = H // 2
L = D // 4
UNITS = 4
ROWS1 = 288
GROUP = 80
ROWS2 = 4 * GROUP
MSG = 208
EDGES = ((0, 112), (112, 48), (160, 48))
norm_epsilon = 1e-05
masked_score = -1e30
MESH = pl.DeviceIdType.MESH
F32 = jnp.float32
BF16 = jnp.bfloat16


def edge_row(lo, la, lv):
    if lo < 6 and la >= 3:
        return (lo * 9 + la - 3) * 2 + lv
    if lo >= 6 and la < 3:
        return 112 + ((lo - 6) * 3 + la) * 2 + lv
    if lo < 6:
        return 160 + (lo * 3 + la) * 2 + lv
    return None


def shifted_row(slo, q, lv):
    return ((q // 6) * 2 + lv) * GROUP + slo * 6 + q % 6


def permutations():
    send = np.zeros((MSG, ROWS1), np.float32)
    own = np.zeros((ROWS2, ROWS1), np.float32)
    arrive = np.zeros((ROWS2, MSG), np.float32)
    back = np.zeros((MSG, ROWS2), np.float32)
    quad_own = np.zeros((4 * GROUP, ROWS2), np.float32)
    quad_edge = np.zeros((4 * GROUP, MSG), np.float32)
    for lo in range(12):
        for la in range(12):
            for lv in range(2):
                first = (la // 6) * 144 + lo * 12 + (la % 6) * 2 + lv
                quad = ((la % 2) * 2 + lo % 2) * GROUP + ((lo // 2) * 6 + la // 2) * 2 + lv
                edge = edge_row(lo, la, lv)
                if edge is None:
                    second = shifted_row(lo - 6, la - 3, lv)
                    own[second, first] = 1
                    quad_own[quad, second] = 1
                else:
                    second = shifted_row((lo - 6) % 12, (la - 3) % 12, lv)
                    send[edge, first] = 1
                    arrive[second, edge] = 1
                    back[edge, second] = 1
                    quad_edge[quad, edge] = 1
    return [p.astype(jnp.bfloat16) for p in (send, own, arrive, back, quad_own, quad_edge)]


def biases():
    pad = np.zeros((GROUP, GROUP), np.float32)
    pad[:, 72:] = masked_score
    cross = np.zeros((GROUP, GROUP), np.float32)
    half = np.arange(72) % 6 < 3
    cross[:72, :72] = np.where(half[:, None] != half[None], masked_score, 0)
    return np.stack([pad, cross])


def normalize(values):
    centred = values - jnp.mean(values, axis=-1, keepdims=True)
    variance = jnp.mean(centred * centred, axis=-1, keepdims=True)
    return (centred * lax.rsqrt(variance + norm_epsilon)).astype(BF16)


def dot_nt(a, b):
    return lax.dot_general(a, b, (((1,), (1,)), ((), ())), preferred_element_type=F32)


def dot(a, b):
    return jnp.dot(a, b, preferred_element_type=F32)


def kernel(
    x_ref, a_ref, bias_ref, send_hbm, own_hbm, arrive_hbm, back_hbm, qown_hbm, qedge_hbm,
    out_ref,
    G, E, piece, qkv, mix, first, second, xn, msg_out, msg_in, ret_out, ret_in,
    p_send, p_own, p_arrive, p_back, p_qown, p_qedge,
    psem, lsem, es, er, zs, zr, p1s, p1r, p2s, p2r, p3s, p3r, ss, sr, hs, hr,
):
    lon, lat = lax.axis_index("lon"), lax.axis_index("lat")
    lons, lats = 4 * Z, 8
    c = lax.rem(lon, 2)
    yh = lax.rem(lon // 2, 2)
    z = lon // 4
    x = lax.rem(lat, 4)
    yl = lat // 4
    y = yh * 2 + yl
    lanes = pl.ds(pl.multiple_of(x * L, L), L)

    def place(x, y, z, c):
        return ((z * 2 + y // 2) * 2 + c, lax.rem(y, 2) * 4 + x)

    def wrap4(v):
        return lax.rem(v + 4, 4)

    sibling = place(x, y, z, 1 - c)
    lon_up, lon_down = lax.rem(lon + 1, lons), lax.rem(lon + lons - 1, lons)
    lat_up, lat_down = lax.rem(lat + 1, lats), lax.rem(lat + lats - 1, lats)
    halo_down = ((lon_down, lat), (lon, lat_down), (lon_down, lat_down))
    halo_up = ((lon_up, lat), (lon, lat_up), (lon_up, lat_up))

    def remote(src, dst, send, recv, device):
        return pltpu.make_async_remote_copy(
            src_ref=src, dst_ref=dst, send_sem=send, recv_sem=recv,
            device_id=device, device_id_type=MESH,
        )

    def drain(ref, sem):
        pltpu.make_async_copy(ref, ref, sem).wait()

    loads = [
        pltpu.make_async_copy(src, dst, psem.at[i])
        for i, (src, dst) in enumerate(
            (
                (send_hbm, p_send), (own_hbm, p_own), (arrive_hbm, p_arrive),
                (back_hbm, p_back), (qown_hbm, p_qown), (qedge_hbm, p_qedge),
            )
        )
    ]
    for load in loads:
        load.start()

    barrier = pltpu.get_barrier_semaphore()

    def greet(device):
        pl.semaphore_signal(barrier, inc=1, device_id=device, device_id_type=MESH)

    greet(sibling)

    @pl.loop(1, Z)
    def _(d):
        greet(place(x, y, lax.rem(z + d, Z), c))

    for d in (1, 2, 3):
        greet(place(wrap4(x + d), y, z, c))
        greet(place(x, wrap4(y + d), z, c))
    for device in halo_down + halo_up:
        greet(device)
    pl.semaphore_wait(barrier, 1 + Z - 1 + 6 + 6)

    eye = (
        lax.broadcasted_iota(jnp.int32, (128, 128), 0)
        == lax.broadcasted_iota(jnp.int32, (128, 128), 1)
    ).astype(F32).astype(BF16)
    turned = dot_nt(eye, a_ref[...])
    E[c] = turned[0:64]
    to_sibling = remote(E.at[c], E.at[c], es, er, sibling)
    to_sibling.start()

    low, high = (yl == 0).astype(F32), (yl == 1).astype(F32)
    core0, core1 = (c == 0).astype(F32), (c == 1).astype(F32)

    def put_piece(u, tile):
        tile = tile.astype(BF16)
        for k in range(4):
            piece[u, k] = tile[:, k * L : (k + 1) * L]

    for m in range(2):
        base = 64 + 32 * m
        put_piece(2 + m, turned[base : base + 16] * low + turned[base + 16 : base + 32] * high)
    to_sibling.wait()
    for s in range(2):
        r0, r1 = E[0, 32 * s : 32 * s + 32], E[1, 32 * s : 32 * s + 32]
        tile = (low * core0) * r0[0:16]
        tile += (low * core1) * jnp.concatenate([r0[16:24], r1[0:8]], axis=0)
        tile += (high * core0) * r1[8:24]
        tile += (high * core1) * jnp.concatenate([r0[24:32], r1[24:32]], axis=0)
        put_piece(s, tile)

    def zsend(u):
        slot = G.at[u, z, yh, yl, c, :, lanes]
        pltpu.make_async_copy(piece.at[u, x], slot, lsem.at[u]).start()

        @pl.loop(1, Z)
        def _(d):
            remote(
                piece.at[u, x], slot, zs.at[u], zr.at[u], place(x, y, lax.rem(z + d, Z), c)
            ).start()

    def halves(u, x, y):
        at = pl.ds(pl.multiple_of(x * L, L), L)
        return (
            G.at[u, 0:H, y // 2, lax.rem(y, 2), c, :, at],
            G.at[u, H:Z, y // 2, lax.rem(y, 2), c, :, at],
        )

    def step_a(u):
        pltpu.make_async_copy(piece.at[u, x], G.at[u, z, yh, yl, c, :, lanes], lsem.at[u]).wait()
        drain(G.at[u, 0 : Z - 1, yh, yl, c, :, lanes], zr.at[u])
        half0, half1 = halves(u, x, y)
        for d in (1, 2, 3):
            remote(half0, half0, p1s.at[u, 0], p1r.at[u, 0], place(wrap4(x + d), y, z, c)).start()
            remote(half1, half1, p1s.at[u, 1], p1r.at[u, 1], place(x, wrap4(y + d), z, c)).start()

    def wide(u, axis, at, z0, n):
        if axis == 0:
            return G.at[u, pl.ds(z0, n), at // 2, lax.rem(at, 2), c]
        span = pl.ds(pl.multiple_of(at * L, L), L)
        return G.at[u, pl.ds(H + z0, n), :, :, c, :, span]

    def along(axis, at):
        return place(x, at, z, c) if axis == 0 else place(at, y, z, c)

    mine = (y, x)

    def step_b(u):
        for half in range(2):
            drain(G.at[u, 0:H, 0, 0, 0, :, 0 : 3 * L], p1r.at[u, half])
        for axis in range(2):
            ref = wide(u, axis, mine[axis], 0, H)
            for way, step in enumerate((1, -1)):
                remote(
                    ref, ref, p2s.at[u, axis, way], p2r.at[u, axis, way],
                    along(axis, wrap4(mine[axis] + step)),
                ).start()

    def step_c(u):
        for axis in range(2):
            for way, step in enumerate((1, -1)):
                drain(wide(u, axis, mine[axis], 0, H), p2r.at[u, axis, way])
                ref = wide(u, axis, wrap4(mine[axis] - step), way * Q, Q)
                remote(
                    ref, ref, p3s.at[u, axis, way], p3r.at[u, axis, way],
                    along(axis, wrap4(mine[axis] + step)),
                ).start()

    def step_d(u):
        for axis in range(2):
            for way in range(2):
                drain(wide(u, axis, mine[axis], 0, Q), p3r.at[u, axis, way])
        ref = G.at[u, :, :, :, c]
        remote(ref, ref, ss.at[u], sr.at[u], sibling).start()

    def step_e(u):
        drain(G.at[u, :, :, :, c], sr.at[u])

    lane = lax.broadcasted_iota(jnp.int32, (1, 128), 1) // 32
    head_f32 = [(lane == h).astype(F32) for h in range(4)]
    head_bf16 = [mask.astype(BF16) for mask in head_f32]

    def project_qkv(u, rows):
        @pl.loop(0, 4)
        def _(i):
            w = G[u, pl.ds(i * (Z // 4), Z // 4)].reshape(Z // 2, 4, 16, D)[:, 0:3]
            r = dot_nt(xn[0:rows], w.reshape(Z // 2 * 48, D)).astype(BF16)
            for j in range(3):
                qkv[i * 3 + j, 0:rows] = r[:, 128 * j : 128 * j + 128]

    def attend(start, n, bias):
        rows = pl.ds(start, n)

        @pl.loop(0, 4)
        def _(g):
            q, k, v = qkv[g, rows], qkv[4 + g, rows], qkv[8 + g, rows]
            stacked = jnp.concatenate([q * mask for mask in head_bf16], axis=0)
            scores = dot_nt(stacked, k) * 32 ** (-0.5)
            if bias is not None:
                scores = scores + bias
            weights = jnp.exp(scores - jnp.max(scores, axis=-1, keepdims=True)).astype(BF16)
            both = dot(weights, jnp.concatenate([v, jnp.ones_like(v)], axis=1))
            total = head_f32[0] * both[0:n]  [:, 0:128]
            norm = head_f32[0] * both[0:n][:, 128:256]
            for h in range(1, 4):
                part = both[h * n : (h + 1) * n]
                total += head_f32[h] * part[:, 0:128]
                norm += head_f32[h] * part[:, 128:256]
            mix[g, rows] = (total / norm).astype(BF16)

    def project_out(u, rows):
        w = G[u].reshape(2 * Z, 4, 16, D)[:, 3].reshape(D, D)
        mixed = jnp.concatenate([mix[g, 0:rows] for g in range(4)], axis=1)
        return dot_nt(mixed, w)

    def exchange(k, src, dst, devices):
        copies = []
        for i, (start, n) in enumerate(EDGES):
            ref, to = src.at[pl.ds(start, n)], dst.at[pl.ds(start, n)]
            copies.append(remote(ref, to, hs.at[k, i], hr.at[k, i], devices[i]))
            copies[-1].start()
        return copies

    zsend(0)
    for u in range(1, UNITS):
        zsend(u)
    xn[0:ROWS1] = normalize(x_ref[...].astype(F32))
    step_a(0)
    step_b(0)
    step_a(1)
    step_c(0)
    step_b(1)
    step_d(0)
    step_a(2)
    step_c(1)
    step_e(0)
    project_qkv(0, ROWS1)
    step_b(2)
    step_d(1)
    attend(0, 144, None)
    step_a(3)
    step_c(2)
    attend(144, 144, None)
    step_b(3)
    first[...] = (x_ref[...].astype(F32) + project_out(0, ROWS1)).astype(BF16)
    for load in loads:
        load.wait()
    msg_out[...] = dot(p_send[...], first[...]).astype(BF16)
    halo = exchange(0, msg_out, msg_in, halo_down)
    step_d(2)
    step_c(3)
    kept = dot(p_own[...], first[...])
    for copy in halo:
        copy.wait()
    second[...] = (kept + dot(p_arrive[...], msg_in[...])).astype(BF16)
    xn[...] = normalize(second[...].astype(F32))
    step_e(1)
    step_d(3)
    project_qkv(1, ROWS2)
    last = (lat == lats - 1).astype(F32)
    for group in range(4):
        bias = bias_ref[0]
        if group >= 2:
            bias = bias + last * bias_ref[1]
        attend(group * GROUP, GROUP, jnp.concatenate([bias] * 4, axis=0))
    second[...] = (second[...].astype(F32) + project_out(1, ROWS2)).astype(BF16)
    ret_out[...] = dot(p_back[...], second[...]).astype(BF16)
    halo = exchange(1, ret_out, ret_in, halo_up)
    kept = dot(p_qown[...], second[...])
    for copy in halo:
        copy.wait()
    quads = kept + dot(p_qedge[...], ret_in[...])
    quads = jnp.concatenate([quads[GROUP * p : GROUP * (p + 1)] for p in range(4)], axis=1)
    quads = normalize(quads)
    step_e(2)
    step_e(3)
    merged = jnp.zeros((GROUP, 2 * D), F32)
    for p in range(4):
        w = G[2 + p // 2].reshape(2 * Z, 2, 32, D)[:, p % 2].reshape(2 * D, D)
        merged += dot_nt(quads[:, p * D : (p + 1) * D], w)
    out_ref[...] = merged[0:72].astype(BF16)

    for u in range(UNITS):
        drain(G.at[u, 0 : Z - 1, yh, yl, c, :, lanes], zs.at[u])
        for half in range(2):
            drain(G.at[u, 0:H, 0, 0, 0, :, 0 : 3 * L], p1s.at[u, half])
        for axis in range(2):
            for way in range(2):
                drain(wide(u, axis, mine[axis], 0, H), p2s.at[u, axis, way])
                drain(wide(u, axis, mine[axis], 0, Q), p3s.at[u, axis, way])
        drain(G.at[u, :, :, :, c], ss.at[u])


def call(tokens, columns):
    perms = permutations()
    vmem = pl.BlockSpec(memory_space=pltpu.VMEM)
    hbm = pl.BlockSpec(memory_space=pl.ANY)
    dma = pltpu.SemaphoreType.DMA
    return pl.pallas_call(
        kernel,
        out_shape=jax.ShapeDtypeStruct((72, 2 * D), BF16),
        in_specs=[vmem] * 3 + [hbm] * 6,
        out_specs=vmem,
        scratch_shapes=[
            pltpu.VMEM((UNITS, Z, 2, 2, 2, 16, D), BF16),
            pltpu.VMEM((2, 64, D), F32),
            pltpu.VMEM((UNITS, 4, 16, L), BF16),
            pltpu.VMEM((12, ROWS2, 128), BF16),
            pltpu.VMEM((4, ROWS2, 128), BF16),
            pltpu.VMEM((ROWS1, D), BF16),
            pltpu.VMEM((ROWS2, D), BF16),
            pltpu.VMEM((ROWS2, D), BF16),
            pltpu.VMEM((MSG, D), BF16),
            pltpu.VMEM((MSG, D), BF16),
            pltpu.VMEM((MSG, D), BF16),
            pltpu.VMEM((MSG, D), BF16),
        ]
        + [pltpu.VMEM(p.shape, BF16) for p in perms]
        + [
            dma((6,)), dma((UNITS,)), dma(()), dma(()), dma((UNITS,)), dma((UNITS,)),
            dma((UNITS, 2)), dma((UNITS, 2)),
            dma((UNITS, 2, 2)), dma((UNITS, 2, 2)), dma((UNITS, 2, 2)), dma((UNITS, 2, 2)),
            dma((UNITS,)), dma((UNITS,)), dma((2, 3)), dma((2, 3)),
        ],
        compiler_params=pltpu.CompilerParams(
            collective_id=0, has_side_effects=True, vmem_limit_bytes=48 * 1024 * 1024
        ),
        name="swin",
    )(tokens, columns, biases(), *perms)


def body(patches, qkv_first, proj_first, qkv_second, proj_second, merge_weight):
    tokens = patches.reshape(12, 2, 6, 2, D).transpose(1, 0, 2, 3, 4).reshape(ROWS1, D)
    merge = [merge_weight[p * D : (p + 1) * D] for p in range(4)]
    columns = jnp.concatenate([qkv_first, proj_first, qkv_second, proj_second] + merge, axis=1)
    merged = call(tokens, columns)
    return merged.reshape(6, 6, 2, 2 * D)


def solution(mesh):
    placed = (
        P("lon", "lat", None, None),
        P(None, "lon"),
        P(None, "lon"),
        P(None, "lon"),
        P(None, "lon"),
        P(None, "lon"),
    )
    return jax.shard_map(
        body, mesh=mesh, in_specs=placed, out_specs=P("lon", "lat", None, None), check_vma=False
    )
```

time: 459 us -> 88.2 us (0.19)
  waiting for transfers between devices: 222 us -> 0 us
  blocking collectives: 166 us -> 0 us
  Pallas kernels: 0 us -> 80 us
  matrix products: 18.9 us -> 0 us
  between operations: 13.5 us -> 0.12 us
  starting transfers between devices: 13.3 us -> 0 us
  other arithmetic: 12.6 us -> 0 us
  local copies, waits for them, and re-layouts: 12 us -> 7.13 us
    all_gather x3 -> x0, waiting for transfers between devices: 208 us -> none  [project(): complete = lax.all_gather(shard, 'lon', axis=1, tiled=True)]
    all_gather x2 -> x0, blocking collectives: 166 us -> none  [project(): complete = lax.all_gather(shard, 'lon', axis=1, tiled=True)]
    pallas_call x0 -> x1, Pallas kernels: none -> 80 us  [call(): pl.pallas_call(kernel, out_shape=jax.ShapeDtypeStruct((72, 2 * D), BF16),...]
    dot_general x11 -> x0, matrix products: 14 us -> none  [the longest x5 8.44 us: project(): product = jnp.dot(activations, complete, preferred_element_type=jnp.float32)]
    ppermute x4 -> x0, starting transfers between devices: 13.2 us -> none  [from_behind(): return lax.ppermute(value, axis, pairs)]
    ppermute x4 -> x0, waiting for transfers between devices: 11.5 us -> none  [from_behind(): return lax.ppermute(value, axis, pairs)]
    reduce_sum x6 -> x0, other arithmetic: 5.08 us -> none  [the longest x3 2.86 us: normalize(): variance = jnp.mean(centred * centred, axis=-1, keepdims=True)]
    sub x2 -> x0, matrix products: 4.87 us -> none  [attend(): weights = jnp.exp(scores - highest)]
  transfers between devices with their start and end apart: 7 -> 0, of which waited for: 6 -> 0; matrix products, arithmetic and copies ran while one was open for 8% -> 0% of each run, Pallas kernels for 0% -> 0%
where the time goes in v1:
time: 88.2 us; the launch traced here: 87.3 us
  Pallas kernels  80 us (91%)
  local copies, waits for them, and re-layouts  7.13 us (8%)
    pallas_call x1, Pallas kernels, call(): pl.pallas_call(kernel, out_shape=jax.ShapeDtypeStruct((72, 2 * D), BF16),...  80 us
    unnamed x28, local copies, waits for them, and re-layouts  4.29 us

profile of v1, /device:TPU:1, one launch (start us, length us, event | category | flops | bytes accessed | tf_op | source)
XLA Modules:
  0.0 87.3 jit_solution(12461402449362453406)
XLA Ops:
  0.0 0.8 fusion
  0.8 0.1 copy.22
  0.9 0.1 copy.20
  1.0 0.1 copy.19
  1.2 0.0 copy-start.8
  1.2 0.1 copy.21
  1.3 0.6 copy-done.8
  1.9 0.0 copy-start.10
  1.9 0.1 copy.15
  2.0 0.6 copy-done.10
  2.6 0.2 copy.16
  2.8 0.6 copy-done.9
  3.3 0.1 copy.17
  3.5 0.6 copy-done.11
  4.0 0.2 copy.18
  4.2 0.0 copy-start.7
  4.2 0.0 copy-start.6
  4.2 0.5 concatenate.3.a_ref
  4.8 0.4 copy-done.7
  5.2 0.2 copy.24
  5.4 0.0 copy-start
  5.4 0.0 copy-start.1
  5.4 0.1 reshape.10.x_ref
  5.5 0.0 copy-done.6
  5.5 0.5 copy-done.2
  6.1 0.1 copy-done.3
  6.2 0.1 copy-done.4
  6.2 0.1 copy-done.5
  6.3 0.1 copy-done
  6.4 0.1 copy-done.1
  6.5 80.0 %swin.1 = bf16[72,1024]{1,0:T(8,128)(2,1)S(1)} custom-call(bf16[288,512]{1,0:T(8,128)(2,1)S(1)} %reshape.10.x_ref, bf16[512,128]{1,0:T(8,128)(2,1)S(1)} %concatenate.3.a_ref, f32[2,80,80]{2,1,0:T(8,128)S(1)} %copy-done.6, bf16[208,288]{1,0:T(8,128)(2,1)S(1)} %copy-done.5, bf16[320,288]{1,0:T(8,128)(2,1)S(1)} %copy-done.1, bf16[320,208]{1,0:T(8,128)(2,1)S(1)} %copy-done.3, ...), custom_call_target="tpu_custom_call" | custom-call | tf_op jit(solution)/shard_map/swin/pallas_call | solution.py:377
  86.6 0.7 reshape.11
  (6 shorter events, 0.0 us)
Async XLA Ops:
  1.2 0.7 copy-start.8
  1.9 0.7 copy-start.10
  2.6 0.7 copy-start.9
  3.3 0.7 copy-start.11
  4.2 1.0 %copy-start.7 = (bf16[12,12,2,512]{3,2,1,0:T(2,128)(2,1)S(1)}, bf16[12,12,2,512]{3,2,1,0:T(2,128)(2,1)}, u32[]{:S(2)}) copy-start(bf16[12,12,2,512]{3,2,1,0:T(2,128)(2,1)} %param.13) | copy-start | bytes 884740
  4.2 1.3 %copy-start.6 = (f32[2,80,80]{2,1,0:T(8,128)S(1)}, f32[2,80,80]{2,1,0:T(8,128)}, u32[]{:S(2)}) copy-start(f32[2,80,80]{2,1,0:T(8,128)} %constant.14.clone.bias_ref) | copy-start | bytes 153604
  5.2 0.9 %copy-start.2 = (bf16[320,208]{1,0:T(8,128)(2,1)S(1)}, bf16[320,208]{1,0:T(8,128)(2,1)}, u32[]{:S(2)}) copy-start(bf16[320,208]{1,0:T(8,128)(2,1)} %constant.20.clone.qedge_hbm) | copy-start | bytes 399364
  5.2 1.0 %copy-start.3 = (bf16[320,208]{1,0:T(8,128)(2,1)S(1)}, bf16[320,208]{1,0:T(8,128)(2,1)}, u32[]{:S(2)}) copy-start(bf16[320,208]{1,0:T(8,128)(2,1)} %constant.17.clone.arrive_hbm) | copy-start | bytes 399364
  5.2 1.1 %copy-start.4 = (bf16[208,320]{1,0:T(8,128)(2,1)S(1)}, bf16[208,320]{1,0:T(8,128)(2,1)}, u32[]{:S(2)}) copy-start(bf16[208,320]{1,0:T(8,128)(2,1)} %constant.18.clone.back_hbm) | copy-start | bytes 399364
  5.2 1.1 %copy-start.5 = (bf16[208,288]{1,0:T(8,128)(2,1)S(1)}, bf16[208,288]{1,0:T(8,128)(2,1)}, u32[]{:S(2)}) copy-start(bf16[208,288]{1,0:T(8,128)(2,1)} %constant.15.clone.send_hbm) | copy-start | bytes 359428
  5.4 1.1 %copy-start = (bf16[320,320]{1,0:T(8,128)(2,1)S(1)}, bf16[320,320]{1,0:T(8,128)(2,1)}, u32[]{:S(2)}) copy-start(bf16[320,320]{1,0:T(8,128)(2,1)} %constant.19.clone.qown_hbm) | copy-start | bytes 614404
  5.4 1.1 %copy-start.1 = (bf16[320,288]{1,0:T(8,128)(2,1)S(1)}, bf16[320,288]{1,0:T(8,128)(2,1)}, u32[]{:S(2)}) copy-start(bf16[320,288]{1,0:T(8,128)(2,1)} %constant.16.clone.own_hbm) | copy-start | bytes 552964

commit v2 on v1

v2 whole, which is shorter than its diff:
```python
import functools

import jax
import jax.numpy as jnp
from jax import lax
from jax.experimental import pallas as pl
from jax.experimental.pallas import tpu as pltpu
from jax.sharding import PartitionSpec as P

D = 512
HEADS = 16
Z = 16
H = Z // 2
Q = H // 2
L = D // 4
SLABS = 4
UNITS = ((0, 1), (1, 1), (2, 2))
ROWS1 = 288
GROUP = 80
ROWS2 = 4 * GROUP
MSG = 208
EDGES = ((0, 112), (112, 48), (160, 48))
norm_epsilon = 1e-05
masked_score = -1e30
EXP2_SCALE = 32 ** (-0.5) * 1.4426950408889634
MESH = pl.DeviceIdType.MESH
F32 = jnp.float32
BF16 = jnp.bfloat16


def split(values, n):
    quotient = jnp.floor((values + 0.5) * (1.0 / n))
    return quotient, values - n * quotient


def both(*conditions):
    return functools.reduce(jnp.logical_and, conditions)


def edge_row(lo, la, lv):
    near = jnp.where(lo < 6, 160 + (lo * 3 + la) * 2 + lv, 112 + ((lo - 6) * 3 + la) * 2 + lv)
    return jnp.where(both(lo < 6, la >= 3), (lo * 9 + la - 3) * 2 + lv, near)


def first_row(lo, la, lv):
    window, rest = split(la, 6)
    return window * 144 + lo * 12 + rest * 2 + lv


def shifted_row(lo, la, lv):
    window, rest = split(jnp.where(la < 3, la + 9, la - 3), 6)
    return (window * 2 + lv) * GROUP + jnp.where(lo < 6, lo + 6, lo - 6) * 6 + rest


def edge_tokens(row):
    start = jnp.where(row < 112, 0, jnp.where(row < 160, 112, 160))
    half, lv = split(row - start, 2)
    lo9, la9 = split(half, 9)
    lo3, la3 = split(half, 3)
    wide = row < 112
    lo = jnp.where(wide, lo9, jnp.where(row < 160, lo3 + 6, lo3))
    la = jnp.where(wide, la9 + 3, la3)
    return lo, la, lv, half < jnp.where(wide, 54, 18)


def shifted_tokens(row):
    group, place = split(row, GROUP)
    window, lv = split(group, 2)
    slo, sla = split(place, 6)
    la = window * 6 + sla + 3
    lo = jnp.where(slo < 6, slo + 6, slo - 6)
    return lo, jnp.where(la < 12, la, la - 12), lv, place < 72


def quad_tokens(row):
    part, place = split(row, GROUP)
    odd_lat, odd_lon = split(part, 2)
    half, lv = split(place, 2)
    i, j = split(half, 6)
    return 2 * i + odd_lon, 2 * j + odd_lat, lv, place < 72


def one_hot(rows, columns, column_of):
    row = lax.broadcasted_iota(jnp.int32, (rows, 1), 0).astype(F32)
    at, valid = column_of(row)
    at = jnp.where(valid, at, -1.0)
    column = lax.broadcasted_iota(jnp.int32, (rows, columns), 1).astype(F32)
    return jnp.where(column == at, 1.0, 0.0).astype(BF16)


def column_send(row):
    lo, la, lv, valid = edge_tokens(row)
    return first_row(lo, la, lv), valid


def column_back(row):
    lo, la, lv, valid = edge_tokens(row)
    return shifted_row(lo, la, lv), valid


def kept(lo, la):
    return both(lo >= 6, la >= 3)


def column_own(row):
    lo, la, lv, valid = shifted_tokens(row)
    return first_row(lo, la, lv), both(valid, kept(lo, la))


def column_arrive(row):
    lo, la, lv, valid = shifted_tokens(row)
    return edge_row(lo, la, lv), both(valid, jnp.logical_not(kept(lo, la)))


def column_quad_own(row):
    lo, la, lv, valid = quad_tokens(row)
    return shifted_row(lo, la, lv), both(valid, kept(lo, la))


def column_quad_edge(row):
    lo, la, lv, valid = quad_tokens(row)
    return edge_row(lo, la, lv), both(valid, jnp.logical_not(kept(lo, la)))


PERMUTATIONS = (
    (MSG, ROWS1, column_send),
    (ROWS2, ROWS1, column_own),
    (ROWS2, MSG, column_arrive),
    (MSG, ROWS2, column_back),
    (4 * GROUP, ROWS2, column_quad_own),
    (4 * GROUP, MSG, column_quad_edge),
)


def normalize(values):
    centred = values - jnp.mean(values, axis=-1, keepdims=True)
    variance = jnp.mean(centred * centred, axis=-1, keepdims=True)
    return (centred * lax.rsqrt(variance + norm_epsilon)).astype(BF16)


def dot_nt(a, b):
    return lax.dot_general(a, b, (((1,), (1,)), ((), ())), preferred_element_type=F32)


def dot(a, b):
    return jnp.dot(a, b, preferred_element_type=F32)


def kernel(
    x_ref, q1_hbm, o1_hbm, q2_hbm, o2_hbm, merge_hbm, out_ref,
    G, E, piece, qkv, mix, first, second, xn, msg_out, msg_in, ret_out, ret_in,
    p_send, p_own, p_arrive, p_back, p_qown, p_qedge, bias_ref, q1, o1, q2, o2, merge,
    wsem, lsem, es, er, zs, zr, p1s, p1r, p2s, p2r, p3s, p3r, ss, sr, hs, hr,
):
    lon, lat = lax.axis_index("lon"), lax.axis_index("lat")
    lons, lats = 4 * Z, 8
    c = lax.rem(lon, 2)
    yh = lax.rem(lon // 2, 2)
    z = lon // 4
    x = lax.rem(lat, 4)
    yl = lat // 4
    y = yh * 2 + yl
    lanes = pl.ds(pl.multiple_of(x * L, L), L)

    def place(x, y, z, c):
        return ((z * 2 + y // 2) * 2 + c, lax.rem(y, 2) * 4 + x)

    def wrap4(v):
        return lax.rem(v + 4, 4)

    sibling = place(x, y, z, 1 - c)
    lon_up, lon_down = lax.rem(lon + 1, lons), lax.rem(lon + lons - 1, lons)
    lat_up, lat_down = lax.rem(lat + 1, lats), lax.rem(lat + lats - 1, lats)
    halo_down = ((lon_down, lat), (lon, lat_down), (lon_down, lat_down))
    halo_up = ((lon_up, lat), (lon, lat_up), (lon_up, lat_up))

    def remote(src, dst, send, recv, device):
        return pltpu.make_async_remote_copy(
            src_ref=src, dst_ref=dst, send_sem=send, recv_sem=recv,
            device_id=device, device_id_type=MESH,
        )

    def drain(ref, sem):
        pltpu.make_async_copy(ref, ref, sem).wait()

    own_columns = ((q1_hbm, q1), (o1_hbm, o1), (q2_hbm, q2), (o2_hbm, o2), (merge_hbm, merge))
    loads = [
        pltpu.make_async_copy(src, dst, wsem.at[i]) for i, (src, dst) in enumerate(own_columns)
    ]
    for load in loads:
        load.start()

    barrier = pltpu.get_barrier_semaphore()

    def greet(device):
        pl.semaphore_signal(barrier, inc=1, device_id=device, device_id_type=MESH)

    def distance(k):
        return 8 + (1 - 2 * lax.rem(k + 1, 2)) * ((k + 1) // 2)

    @pl.loop(0, Z - 1)
    def _(k):
        greet(place(x, y, lax.rem(z + distance(k), Z), c))

    for d in (2, 1, 3):
        greet(place(wrap4(x + d), y, z, c))
        greet(place(x, wrap4(y + d), z, c))
    for device in halo_down + halo_up:
        greet(device)
    greet(sibling)

    for load in loads:
        load.wait()
    for ref, start, n in ((q1, 0, 24), (o1, 24, 8), (q2, 32, 24), (o2, 56, 8)):
        E[c, start : start + n] = ref[...].astype(F32)
    pl.semaphore_wait(barrier, 1 + Z - 1 + 6 + 6)
    to_sibling = remote(E.at[c], E.at[c], es, er, sibling)
    to_sibling.start()

    low, high = (yl == 0).astype(F32), (yl == 1).astype(F32)
    core0, core1 = (c == 0).astype(F32), (c == 1).astype(F32)

    def put_piece(u, tile):
        tile = tile.astype(BF16)
        for k in range(4):
            piece[u, k] = tile[:, k * L : (k + 1) * L]

    for m in range(2):
        rows = merge[:, 2 * m * D : 2 * (m + 1) * D].astype(F32)
        put_piece(2 + m, rows[:, 0:D] * low + rows[:, D : 2 * D] * high)
    to_sibling.wait()
    for s in range(2):
        r0, r1 = E[0, 32 * s : 32 * s + 32], E[1, 32 * s : 32 * s + 32]
        tile = (low * core0) * r0[0:16]
        tile += (low * core1) * jnp.concatenate([r0[16:24], r1[0:8]], axis=0)
        tile += (high * core0) * r1[8:24]
        tile += (high * core1) * jnp.concatenate([r0[24:32], r1[24:32]], axis=0)
        put_piece(s, tile)

    def of(u):
        return pl.ds(*UNITS[u])

    def home(u):
        return G.at[of(u), z, yh, yl, c, :, lanes]

    def zsend(u):
        src, slot = piece.at[of(u), x], home(u)
        pltpu.make_async_copy(src, slot, lsem.at[u]).start()

        @pl.loop(0, Z - 1)
        def _(k):
            device = place(x, y, lax.rem(z + distance(k), Z), c)
            remote(src, slot, zs.at[u], zr.at[u], device).start()

    def zbytes(u):
        return G.at[of(u), 0 : Z - 1, yh, yl, c, :, lanes]

    def p1bytes(u):
        return G.at[of(u), 0:H, 0, 0, 0, :, 0 : 3 * L]

    def step_a(u):
        pltpu.make_async_copy(piece.at[of(u), x], home(u), lsem.at[u]).wait()
        drain(zbytes(u), zr.at[u])
        half0 = G.at[of(u), 0:H, yh, yl, c, :, lanes]
        half1 = G.at[of(u), H:Z, yh, yl, c, :, lanes]
        for d in (2, 1, 3):
            remote(half0, half0, p1s.at[u, 0], p1r.at[u, 0], place(wrap4(x + d), y, z, c)).start()
            remote(half1, half1, p1s.at[u, 1], p1r.at[u, 1], place(x, wrap4(y + d), z, c)).start()

    def wide(u, axis, at, z0, n):
        if axis == 0:
            return G.at[of(u), pl.ds(z0, n), at // 2, lax.rem(at, 2), c]
        span = pl.ds(pl.multiple_of(at * L, L), L)
        return G.at[of(u), pl.ds(H + z0, n), :, :, c, :, span]

    def along(axis, at):
        return place(x, at, z, c) if axis == 0 else place(at, y, z, c)

    mine = (y, x)

    def to_core(u, axis, at):
        ref = wide(u, axis, at, 0, H)
        remote(ref, ref, ss.at[u], sr.at[u], sibling).start()

    def step_b(u):
        for axis in range(2):
            drain(p1bytes(u), p1r.at[u, axis])
            ref = wide(u, axis, mine[axis], 0, H)
            for way, step in enumerate((1, -1)):
                remote(
                    ref, ref, p2s.at[u, axis, way], p2r.at[u, axis, way],
                    along(axis, wrap4(mine[axis] + step)),
                ).start()
        if u == 0:
            for axis in range(2):
                to_core(u, axis, mine[axis])

    def step_c(u):
        for axis in range(2):
            for way, step in enumerate((1, -1)):
                drain(wide(u, axis, mine[axis], 0, H), p2r.at[u, axis, way])
                ref = wide(u, axis, wrap4(mine[axis] - step), way * Q, Q)
                remote(
                    ref, ref, p3s.at[u, axis, way], p3r.at[u, axis, way],
                    along(axis, wrap4(mine[axis] + step)),
                ).start()
        if u == 0:
            for axis in range(2):
                for step in (1, -1):
                    to_core(u, axis, wrap4(mine[axis] + step))

    def step_d(u):
        for axis in range(2):
            for way in range(2):
                drain(wide(u, axis, mine[axis], 0, Q), p3r.at[u, axis, way])
            if u == 0:
                to_core(u, axis, wrap4(mine[axis] + 2))
        if u > 0:
            ref = G.at[of(u), :, :, :, c]
            remote(ref, ref, ss.at[u], sr.at[u], sibling).start()

    def step_e(u):
        drain(G.at[of(u), :, :, :, c], sr.at[u])

    lane = lax.broadcasted_iota(jnp.int32, (1, 128), 1) // 32
    head_f32 = [(lane == h).astype(F32) for h in range(4)]
    head_bf16 = [mask.astype(BF16) for mask in head_f32]

    def project_qkv(u, rows):
        @pl.loop(0, 4)
        def _(i):
            w = G[u, pl.ds(i * (Z // 4), Z // 4)].reshape(Z // 2, 4, 16, D)[:, 0:3]
            r = dot_nt(xn[0:rows], w.reshape(Z // 2 * 48, D)).astype(BF16)
            for j in range(3):
                qkv[i * 3 + j, 0:rows] = r[:, 128 * j : 128 * j + 128]

    def attend(start, n, bias):
        rows = pl.ds(start, n)
        for g in range(4):
            q, k, v = qkv[g, rows], qkv[4 + g, rows], qkv[8 + g, rows]
            stacked = jnp.concatenate([q * mask for mask in head_bf16], axis=0)
            scores = dot_nt(stacked, k)
            if bias is not None:
                scores = scores + bias
            highest = jnp.max(scores, axis=-1, keepdims=True)
            weights = jnp.exp2((scores - highest) * EXP2_SCALE).astype(BF16)
            summed = dot(weights, jnp.concatenate([v, jnp.ones_like(v)], axis=1))
            total = head_f32[0] * summed[0:n, 0:128]
            norm = head_f32[0] * summed[0:n, 128:256]
            for h in range(1, 4):
                total += head_f32[h] * summed[h * n : (h + 1) * n, 0:128]
                norm += head_f32[h] * summed[h * n : (h + 1) * n, 128:256]
            mix[g, rows] = (total / norm).astype(BF16)

    def project_out(u, rows):
        w = G[u].reshape(2 * Z, 4, 16, D)[:, 3].reshape(D, D)
        mixed = jnp.concatenate([mix[g, 0:rows] for g in range(4)], axis=1)
        return dot_nt(mixed, w)

    def exchange(k, src, dst, devices):
        copies = []
        for i, (start, n) in enumerate(EDGES):
            ref, to = src.at[pl.ds(start, n)], dst.at[pl.ds(start, n)]
            copies.append(remote(ref, to, hs.at[k, i], hr.at[k, i], devices[i]))
            copies[-1].start()
        return copies

    zsend(0)
    for ref, (rows, columns, column_of) in zip(
        (p_send, p_own, p_arrive, p_back, p_qown, p_qedge), PERMUTATIONS
    ):
        ref[...] = one_hot(rows, columns, column_of)
    row = lax.broadcasted_iota(jnp.int32, (GROUP, GROUP), 0).astype(F32)
    column = lax.broadcasted_iota(jnp.int32, (GROUP, GROUP), 1).astype(F32)
    bias_ref[0] = jnp.where(column < 72, 0.0, masked_score)
    north = split(row, 6)[1] < 3
    bias_ref[1] = jnp.where(north == (split(column, 6)[1] < 3), 0.0, masked_score)
    xn[0:ROWS1] = normalize(x_ref[...].astype(F32))
    step_a(0)
    zsend(1)
    zsend(2)
    step_b(0)
    step_c(0)
    step_a(1)
    step_d(0)
    step_b(1)
    step_a(2)
    step_e(0)
    project_qkv(0, ROWS1)
    attend(0, 144, None)
    step_c(1)
    attend(144, 144, None)
    step_b(2)
    first[...] = (x_ref[...].astype(F32) + project_out(0, ROWS1)).astype(BF16)
    msg_out[...] = dot(p_send[...], first[...]).astype(BF16)
    halo_first = exchange(0, msg_out, msg_in, halo_down)
    stay = dot(p_own[...], first[...])
    step_d(1)
    for copy in halo_first:
        copy.wait_recv()
    second[...] = (stay + dot(p_arrive[...], msg_in[...])).astype(BF16)
    xn[...] = normalize(second[...].astype(F32))
    step_e(1)
    project_qkv(1, ROWS2)
    step_c(2)
    last = (lat == lats - 1).astype(F32)

    def attend_shifted(group):
        bias = bias_ref[0] + (last * (group >= 2).astype(F32)) * bias_ref[1]
        attend(pl.multiple_of(group * GROUP, 16), GROUP, jnp.concatenate([bias] * 4, axis=0))

    pl.loop(0, 4)(attend_shifted)
    step_d(2)
    second[...] = (second[...].astype(F32) + project_out(1, ROWS2)).astype(BF16)
    ret_out[...] = dot(p_back[...], second[...]).astype(BF16)
    halo_second = exchange(1, ret_out, ret_in, halo_up)
    stay = dot(p_qown[...], second[...])
    for copy in halo_second:
        copy.wait_recv()
    quads = stay + dot(p_qedge[...], ret_in[...])
    quads = jnp.concatenate([quads[GROUP * p : GROUP * (p + 1)] for p in range(4)], axis=1)
    quads = normalize(quads)
    step_e(2)
    merged = jnp.zeros((GROUP, 2 * D), F32)
    for p in range(4):
        w = G[2 + p // 2].reshape(2 * Z, 2, 32, D)[:, p % 2].reshape(2 * D, D)
        merged += dot_nt(quads[:, p * D : (p + 1) * D], w)
    out_ref[...] = merged[0:72].astype(BF16)

    for copy in halo_first + halo_second:
        copy.wait_send()
    for u in range(len(UNITS)):
        drain(zbytes(u), zs.at[u])
        for axis in range(2):
            drain(p1bytes(u), p1s.at[u, axis])
            for way in range(2):
                drain(wide(u, axis, mine[axis], 0, H), p2s.at[u, axis, way])
                drain(wide(u, axis, mine[axis], 0, Q), p3s.at[u, axis, way])
        drain(G.at[of(u), :, :, :, c], ss.at[u])


def call(tokens, *columns):
    vmem = pl.BlockSpec(memory_space=pltpu.VMEM)
    dma = pltpu.SemaphoreType.DMA
    return pl.pallas_call(
        kernel,
        out_shape=jax.ShapeDtypeStruct((72, 2 * D), BF16),
        in_specs=[vmem] + [pl.BlockSpec(memory_space=pl.ANY)] * 5,
        out_specs=vmem,
        scratch_shapes=[
            pltpu.VMEM((SLABS, Z, 2, 2, 2, 16, D), BF16),
            pltpu.VMEM((2, 64, D), F32),
            pltpu.VMEM((SLABS, 4, 16, L), BF16),
            pltpu.VMEM((12, ROWS2, 128), BF16),
            pltpu.VMEM((4, ROWS2, 128), BF16),
            pltpu.VMEM((ROWS1, D), BF16),
            pltpu.VMEM((ROWS2, D), BF16),
            pltpu.VMEM((ROWS2, D), BF16),
            pltpu.VMEM((MSG, D), BF16),
            pltpu.VMEM((MSG, D), BF16),
            pltpu.VMEM((MSG, D), BF16),
            pltpu.VMEM((MSG, D), BF16),
        ]
        + [pltpu.VMEM(p[:2], BF16) for p in PERMUTATIONS]
        + [
            pltpu.VMEM((2, GROUP, GROUP), F32),
            pltpu.VMEM((24, D), BF16),
            pltpu.VMEM((8, D), BF16),
            pltpu.VMEM((24, D), BF16),
            pltpu.VMEM((8, D), BF16),
            pltpu.VMEM((16, 4 * D), BF16),
            dma((5,)),
            dma((len(UNITS),)), dma(()), dma(()), dma((len(UNITS),)), dma((len(UNITS),)),
            dma((len(UNITS), 2)), dma((len(UNITS), 2)),
            dma((len(UNITS), 2, 2)), dma((len(UNITS), 2, 2)), dma((len(UNITS), 2, 2)), dma((len(UNITS), 2, 2)),
            dma((len(UNITS),)), dma((len(UNITS),)), dma((2, 3)), dma((2, 3)),
        ],
        compiler_params=pltpu.CompilerParams(
            collective_id=0, has_side_effects=True, vmem_limit_bytes=48 * 1024 * 1024
        ),
        name="swin",
    )(tokens, *columns)


def body(patches, qkv_first, proj_first, qkv_second, proj_second, merge_weight):
    tokens = patches.reshape(12, 2, 6, 2, D).transpose(1, 0, 2, 3, 4).reshape(ROWS1, D)
    merged = call(
        tokens, qkv_first.T, proj_first.T, qkv_second.T, proj_second.T, merge_weight.T
    )
    return merged.reshape(6, 6, 2, 2 * D)


def solution(mesh):
    placed = (
        P("lon", "lat", None, None),
        P(None, "lon"),
        P(None, "lon"),
        P(None, "lon"),
        P(None, "lon"),
        P(None, "lon"),
    )
    return jax.shard_map(
        body, mesh=mesh, in_specs=placed, out_specs=P("lon", "lat", None, None), check_vma=False
    )
```

time: 88.2 us -> 75.4 us (0.85)
  Pallas kernels: 80 us -> 72.4 us
  local copies, waits for them, and re-layouts: 7.13 us -> 2.69 us
    pallas_call x1, Pallas kernels: 80 us -> 72.4 us  [call(): pl.pallas_call(kernel, out_shape=jax.ShapeDtypeStruct((72, 2 * D), BF16),...]
    unnamed x28 -> x10, local copies, waits for them, and re-layouts: 4.29 us -> 0.69 us
    slice x5 -> x0, local copies, waits for them, and re-layouts: 1.26 us -> none  [body(): merge = [merge_weight[p * D:(p + 1) * D] for p in range(4)]]
    reshape x2, local copies, waits for them, and re-layouts: 0.32 us -> 1.28 us  [body(): patches.reshape(12, 2, 6, 2, D).transpose(1, 0, 2, 3, 4).reshape(ROWS1, D)]
where the time goes in v2:
time: 75.4 us; the launch traced here: 75.2 us
  Pallas kernels  72.4 us (96%)
  local copies, waits for them, and re-layouts  2.69 us (4%)
    pallas_call x1, Pallas kernels, call(): pl.pallas_call(kernel, out_shape=jax.ShapeDtypeStruct((72, 2 * D), BF16),...  72.4 us

profile of v2, /device:TPU:1, one launch (start us, length us, event | category | flops | bytes accessed | tf_op | source)
XLA Modules:
  0.0 75.2 jit_solution(16479574664867893453)
XLA Ops:
  0.0 1.2 %copy.9 = bf16[12,2,6,2,512]{4,3,2,0,1:T(2,128)(2,1)S(1)} copy(bf16[12,2,6,2,512]{4,3,2,1,0:T(2,128)(2,1)} %bitcast.15) | data formatting | bytes 589824 | tf_op jit(solution)/shard_map/reshape | solution.py:486
  1.2 0.0 copy-start
  1.2 0.0 copy-start.1
  1.2 0.0 copy-start.2
  1.2 0.0 copy-start.3
  1.2 0.0 copy-start.4
  1.2 0.1 reshape.10.x_ref
  1.4 0.7 copy-done
  2.0 0.0 copy-done.1
  2.0 0.0 copy-done.2
  2.0 0.0 copy-done.3
  2.0 0.0 copy-done.4
  2.0 72.4 %swin.1 = bf16[72,1024]{1,0:T(8,128)(2,1)S(1)} custom-call(bf16[288,512]{1,0:T(8,128)(2,1)S(1)} %reshape.10.x_ref, bf16[24,512]{1,0:T(8,128)(2,1)S(1)} %bitcast.10, bf16[8,512]{1,0:T(8,128)(2,1)S(1)} %bitcast.12, bf16[24,512]{1,0:T(8,128)(2,1)S(1)} %bitcast.11, bf16[8,512]{1,0:T(8,128)(2,1)S(1)} %bitcast.13, bf16[16,2048]{1,0:T(8,128)(2,1)S(1)} %bitcast.9), custom_call_target="tpu_custom_call" | custom-call | tf_op jit(solution)/shard_map/swin/pallas_call | solution.py:445
  74.5 0.7 reshape.11
Async XLA Ops:
  1.2 0.8 %copy-start = (bf16[2048,16]{0,1:T(8,128)(2,1)S(1)}, bf16[2048,16]{0,1:T(8,128)(2,1)}, u32[]{:S(2)}) copy-start(bf16[2048,16]{0,1:T(8,128)(2,1)} %param.11) | copy-start | bytes 196612
  1.2 0.8 %copy-start.1 = (bf16[512,24]{0,1:T(8,128)(2,1)S(1)}, bf16[512,24]{0,1:T(8,128)(2,1)}, u32[]{:S(2)}) copy-start(bf16[512,24]{0,1:T(8,128)(2,1)} %param.7) | copy-start | bytes 73732
  1.2 0.8 %copy-start.2 = (bf16[512,24]{0,1:T(8,128)(2,1)S(1)}, bf16[512,24]{0,1:T(8,128)(2,1)}, u32[]{:S(2)}) copy-start(bf16[512,24]{0,1:T(8,128)(2,1)} %param.9) | copy-start | bytes 73732
  1.2 0.8 %copy-start.3 = (bf16[512,8]{0,1:T(8,128)(2,1)S(1)}, bf16[512,8]{0,1:T(8,128)(2,1)}, u32[]{:S(2)}) copy-start(bf16[512,8]{0,1:T(8,128)(2,1)} %param.8) | copy-start | bytes 24580
  1.2 0.8 %copy-start.4 = (bf16[512,8]{0,1:T(8,128)(2,1)S(1)}, bf16[512,8]{0,1:T(8,128)(2,1)}, u32[]{:S(2)}) copy-start(bf16[512,8]{0,1:T(8,128)(2,1)} %param.10) | copy-start | bytes 24580

commit v3 on v2

--- a/solution.py
+++ b/solution.py
@@ -15,6 +15,8 @@
 L = D // 4
 SLABS = 4
 UNITS = ((0, 1), (1, 1), (2, 2))
+DIRECT = (True, False, False)
+WAYS = ((0, 1), (1, -1), (2, 2))
 ROWS1 = 288
 GROUP = 80
 ROWS2 = 4 * GROUP
@@ -147,9 +149,9 @@
 
 
 def kernel(
-    x_ref, q1_hbm, o1_hbm, q2_hbm, o2_hbm, merge_hbm, out_ref,
+    x_hbm, q1_hbm, o1_hbm, q2_hbm, o2_hbm, merge_hbm, out_ref,
     G, E, piece, qkv, mix, first, second, xn, msg_out, msg_in, ret_out, ret_in,
-    p_send, p_own, p_arrive, p_back, p_qown, p_qedge, bias_ref, q1, o1, q2, o2, merge,
+    p_send, p_own, p_arrive, p_back, p_qown, p_qedge, bias_ref, q1, o1, q2, o2, merge, grid, x_ref,
     wsem, lsem, es, er, zs, zr, p1s, p1r, p2s, p2r, p3s, p3r, ss, sr, hs, hr,
 ):
     lon, lat = lax.axis_index("lon"), lax.axis_index("lat")
@@ -184,6 +186,8 @@
         pltpu.make_async_copy(ref, ref, sem).wait()
 
     own_columns = ((q1_hbm, q1), (o1_hbm, o1), (q2_hbm, q2), (o2_hbm, o2), (merge_hbm, merge))
+    grid_load = pltpu.make_async_copy(x_hbm, grid, wsem.at[5])
+    grid_load.start()
     loads = [
         pltpu.make_async_copy(src, dst, wsem.at[i]) for i, (src, dst) in enumerate(own_columns)
     ]
@@ -286,38 +290,36 @@
         for axis in range(2):
             drain(p1bytes(u), p1r.at[u, axis])
             ref = wide(u, axis, mine[axis], 0, H)
-            for way, step in enumerate((1, -1)):
+            for way, step in WAYS[: 3 if DIRECT[u] else 2]:
                 remote(
                     ref, ref, p2s.at[u, axis, way], p2r.at[u, axis, way],
                     along(axis, wrap4(mine[axis] + step)),
                 ).start()
-        if u == 0:
-            for axis in range(2):
-                to_core(u, axis, mine[axis])
+        for axis in range(2):
+            to_core(u, axis, mine[axis])
 
     def step_c(u):
         for axis in range(2):
-            for way, step in enumerate((1, -1)):
+            for way, step in WAYS[:2]:
                 drain(wide(u, axis, mine[axis], 0, H), p2r.at[u, axis, way])
-                ref = wide(u, axis, wrap4(mine[axis] - step), way * Q, Q)
-                remote(
-                    ref, ref, p3s.at[u, axis, way], p3r.at[u, axis, way],
-                    along(axis, wrap4(mine[axis] + step)),
-                ).start()
-        if u == 0:
-            for axis in range(2):
-                for step in (1, -1):
-                    to_core(u, axis, wrap4(mine[axis] + step))
+                if not DIRECT[u]:
+                    ref = wide(u, axis, wrap4(mine[axis] - step), way * Q, Q)
+                    remote(
+                        ref, ref, p3s.at[u, axis, way], p3r.at[u, axis, way],
+                        along(axis, wrap4(mine[axis] + step)),
+                    ).start()
+        for axis in range(2):
+            for way, step in WAYS[:2]:
+                to_core(u, axis, wrap4(mine[axis] + step))
 
     def step_d(u):
         for axis in range(2):
-            for way in range(2):
-                drain(wide(u, axis, mine[axis], 0, Q), p3r.at[u, axis, way])
-            if u == 0:
-                to_core(u, axis, wrap4(mine[axis] + 2))
-        if u > 0:
-            ref = G.at[of(u), :, :, :, c]
-            remote(ref, ref, ss.at[u], sr.at[u], sibling).start()
+            if DIRECT[u]:
+                drain(wide(u, axis, mine[axis], 0, H), p2r.at[u, axis, 2])
+            else:
+                for way in range(2):
+                    drain(wide(u, axis, mine[axis], 0, Q), p3r.at[u, axis, way])
+            to_core(u, axis, wrap4(mine[axis] + 2))
 
     def step_e(u):
         drain(G.at[of(u), :, :, :, c], sr.at[u])
@@ -327,12 +329,11 @@
     head_bf16 = [mask.astype(BF16) for mask in head_f32]
 
     def project_qkv(u, rows):
-        @pl.loop(0, 4)
-        def _(i):
-            w = G[u, pl.ds(i * (Z // 4), Z // 4)].reshape(Z // 2, 4, 16, D)[:, 0:3]
-            r = dot_nt(xn[0:rows], w.reshape(Z // 2 * 48, D)).astype(BF16)
-            for j in range(3):
-                qkv[i * 3 + j, 0:rows] = r[:, 128 * j : 128 * j + 128]
+        w = G[u].reshape(2 * Z, 4, 16, D)[:, 0:3].reshape(3 * D, D)
+        for i in range(3):
+            r = dot_nt(xn[0:rows], w[D * i : D * (i + 1)]).astype(BF16)
+            for j in range(4):
+                qkv[i * 4 + j, 0:rows] = r[:, 128 * j : 128 * j + 128]
 
     def attend(start, n, bias):
         rows = pl.ds(start, n)
@@ -375,26 +376,29 @@
     bias_ref[0] = jnp.where(column < 72, 0.0, masked_score)
     north = split(row, 6)[1] < 3
     bias_ref[1] = jnp.where(north == (split(column, 6)[1] < 3), 0.0, masked_score)
+    grid_load.wait()
+    for w in range(2):
+        x_ref[144 * w : 144 * w + 144] = grid[:, 6 * w : 6 * w + 6].reshape(144, D)
     xn[0:ROWS1] = normalize(x_ref[...].astype(F32))
+    zsend(1)
     step_a(0)
-    zsend(1)
     zsend(2)
     step_b(0)
+    step_a(1)
     step_c(0)
-    step_a(1)
     step_d(0)
     step_b(1)
     step_a(2)
     step_e(0)
     project_qkv(0, ROWS1)
     attend(0, 144, None)
-    step_c(1)
     attend(144, 144, None)
-    step_b(2)
     first[...] = (x_ref[...].astype(F32) + project_out(0, ROWS1)).astype(BF16)
     msg_out[...] = dot(p_send[...], first[...]).astype(BF16)
     halo_first = exchange(0, msg_out, msg_in, halo_down)
     stay = dot(p_own[...], first[...])
+    step_c(1)
+    step_b(2)
     step_d(1)
     for copy in halo_first:
         copy.wait_recv()
@@ -402,19 +406,24 @@
     xn[...] = normalize(second[...].astype(F32))
     step_e(1)
     project_qkv(1, ROWS2)
+    last = (lat == lats - 1).astype(F32)
+
+    def attend_shifted(group):
+        bias = bias_ref[0]
+        if group >= 2:
+            bias = bias + last * bias_ref[1]
+        attend(group * GROUP, GROUP, jnp.concatenate([bias] * 4, axis=0))
+
+    for group in range(2):
+        attend_shifted(group)
     step_c(2)
-    last = (lat == lats - 1).astype(F32)
-
-    def attend_shifted(group):
-        bias = bias_ref[0] + (last * (group >= 2).astype(F32)) * bias_ref[1]
-        attend(pl.multiple_of(group * GROUP, 16), GROUP, jnp.concatenate([bias] * 4, axis=0))
-
-    pl.loop(0, 4)(attend_shifted)
-    step_d(2)
+    for group in range(2, 4):
+        attend_shifted(group)
     second[...] = (second[...].astype(F32) + project_out(1, ROWS2)).astype(BF16)
     ret_out[...] = dot(p_back[...], second[...]).astype(BF16)
     halo_second = exchange(1, ret_out, ret_in, halo_up)
     stay = dot(p_qown[...], second[...])
+    step_d(2)
     for copy in halo_second:
         copy.wait_recv()
     quads = stay + dot(p_qedge[...], ret_in[...])
@@ -433,9 +442,11 @@
         drain(zbytes(u), zs.at[u])
         for axis in range(2):
             drain(p1bytes(u), p1s.at[u, axis])
-            for way in range(2):
+            for way in range(3 if DIRECT[u] else 2):
                 drain(wide(u, axis, mine[axis], 0, H), p2s.at[u, axis, way])
-                drain(wide(u, axis, mine[axis], 0, Q), p3s.at[u, axis, way])
+            if not DIRECT[u]:
+                for way in range(2):
+                    drain(wide(u, axis, mine[axis], 0, Q), p3s.at[u, axis, way])
         drain(G.at[of(u), :, :, :, c], ss.at[u])
 
 
@@ -445,7 +456,7 @@
     return pl.pallas_call(
         kernel,
         out_shape=jax.ShapeDtypeStruct((72, 2 * D), BF16),
-        in_specs=[vmem] + [pl.BlockSpec(memory_space=pl.ANY)] * 5,
+        in_specs=[pl.BlockSpec(memory_space=pl.ANY)] * 6,
         out_specs=vmem,
         scratch_shapes=[
             pltpu.VMEM((SLABS, Z, 2, 2, 2, 16, D), BF16),
@@ -469,23 +480,24 @@
             pltpu.VMEM((24, D), BF16),
             pltpu.VMEM((8, D), BF16),
             pltpu.VMEM((16, 4 * D), BF16),
-            dma((5,)),
+            pltpu.VMEM((12, 12, 2, D), BF16),
+            pltpu.VMEM((ROWS1, D), BF16),
+            dma((6,)),
             dma((len(UNITS),)), dma(()), dma(()), dma((len(UNITS),)), dma((len(UNITS),)),
             dma((len(UNITS), 2)), dma((len(UNITS), 2)),
-            dma((len(UNITS), 2, 2)), dma((len(UNITS), 2, 2)), dma((len(UNITS), 2, 2)), dma((len(UNITS), 2, 2)),
+            dma((len(UNITS), 2, 3)), dma((len(UNITS), 2, 3)), dma((len(UNITS), 2, 2)), dma((len(UNITS), 2, 2)),
             dma((len(UNITS),)), dma((len(UNITS),)), dma((2, 3)), dma((2, 3)),
         ],
         compiler_params=pltpu.CompilerParams(
-            collective_id=0, has_side_effects=True, vmem_limit_bytes=48 * 1024 * 1024
+            collective_id=0, has_side_effects=True, vmem_limit_bytes=60 * 1024 * 1024
         ),
         name="swin",
     )(tokens, *columns)
 
 
 def body(patches, qkv_first, proj_first, qkv_second, proj_second, merge_weight):
-    tokens = patches.reshape(12, 2, 6, 2, D).transpose(1, 0, 2, 3, 4).reshape(ROWS1, D)
     merged = call(
-        tokens, qkv_first.T, proj_first.T, qkv_second.T, proj_second.T, merge_weight.T
+        patches, qkv_first.T, proj_first.T, qkv_second.T, proj_second.T, merge_weight.T
     )
     return merged.reshape(6, 6, 2, 2 * D)
 

time: 75.4 us -> 65.4 us (0.87)
  Pallas kernels: 72.4 us -> 63.6 us
  local copies, waits for them, and re-layouts: 2.69 us -> 1.63 us
    pallas_call x1, Pallas kernels: 72.4 us -> 63.6 us  [call(): pl.pallas_call(kernel, out_shape=jax.ShapeDtypeStruct((72, 2 * D), BF16),...]
    reshape x2 -> x0, local copies, waits for them, and re-layouts: 1.28 us -> none  [body(): patches.reshape(12, 2, 6, 2, D).transpose(1, 0, 2, 3, 4).reshape(ROWS1, D)]
    reshape x1, local copies, waits for them, and re-layouts: 0.72 us -> 1.63 us  [body(): return merged.reshape(6, 6, 2, 2 * D)]
where the time goes in v3:
time: 65.4 us; the launch traced here: 65.2 us
  Pallas kernels  63.6 us (97%)
  local copies, waits for them, and re-layouts  1.63 us (2%)
    pallas_call x1, Pallas kernels, call(): pl.pallas_call(kernel, out_shape=jax.ShapeDtypeStruct((72, 2 * D), BF16),...  63.6 us
    reshape x1, local copies, waits for them, and re-layouts, body(): return merged.reshape(6, 6, 2, 2 * D)  1.63 us

profile of v3, /device:TPU:1, one launch (start us, length us, event | category | flops | bytes accessed | tf_op | source)
XLA Modules:
  0.0 65.2 jit_solution(3813390259438397223)
XLA Ops:
  0.0 63.6 %swin.1 = bf16[72,1024]{1,0:T(8,128)(2,1)} custom-call(bf16[12,12,2,512]{3,2,1,0:T(2,128)(2,1)} %x_hbm.1, bf16[24,512]{1,0:T(8,128)(2,1)} %bitcast.6, bf16[8,512]{1,0:T(8,128)(2,1)} %bitcast.8, bf16[24,512]{1,0:T(8,128)(2,1)} %bitcast.7, bf16[8,512]{1,0:T(8,128)(2,1)} %bitcast.9, bf16[16,2048]{1,0:T(8,128)(2,1)} %bitcast.5), custom_call_target="tpu_custom_call" | custom-call | tf_op jit(solution)/shard_map/swin/pallas_call | solution.py:456
  63.6 1.6 %reshape.3 = bf16[6,6,2,1024]{3,2,1,0:T(2,128)(2,1)} reshape(bf16[72,1024]{1,0:T(8,128)(2,1)} %swin.1) | data formatting | bytes 294912 | tf_op jit(solution)/shard_map/reshape | solution.py:502

commit v4 on v3

--- a/solution.py
+++ b/solution.py
@@ -360,7 +360,8 @@
 
     def exchange(k, src, dst, devices):
         copies = []
-        for i, (start, n) in enumerate(EDGES):
+        for i in (2, 1, 0):
+            start, n = EDGES[i]
             ref, to = src.at[pl.ds(start, n)], dst.at[pl.ds(start, n)]
             copies.append(remote(ref, to, hs.at[k, i], hr.at[k, i], devices[i]))
             copies[-1].start()

time: 65.4 us -> 64.8 us (level)
  no operation moved by 1% of the time
where the time goes in v4:
time: 64.8 us; the launch traced here: 64.6 us
  Pallas kernels  63 us (97%)
  local copies, waits for them, and re-layouts  1.63 us (3%)
    pallas_call x1, Pallas kernels, call(): pl.pallas_call(kernel, out_shape=jax.ShapeDtypeStruct((72, 2 * D), BF16),...  63 us
    reshape x1, local copies, waits for them, and re-layouts, body(): return merged.reshape(6, 6, 2, 2 * D)  1.63 us

profile of v4, /device:TPU:1, one launch (start us, length us, event | category | flops | bytes accessed | tf_op | source)
XLA Modules:
  0.0 64.6 jit_solution(14422374435401554375)
XLA Ops:
  0.0 63.0 %swin.1 = bf16[72,1024]{1,0:T(8,128)(2,1)} custom-call(bf16[12,12,2,512]{3,2,1,0:T(2,128)(2,1)} %x_hbm.1, bf16[24,512]{1,0:T(8,128)(2,1)} %bitcast.6, bf16[8,512]{1,0:T(8,128)(2,1)} %bitcast.8, bf16[24,512]{1,0:T(8,128)(2,1)} %bitcast.7, bf16[8,512]{1,0:T(8,128)(2,1)} %bitcast.9, bf16[16,2048]{1,0:T(8,128)(2,1)} %bitcast.5), custom_call_target="tpu_custom_call" | custom-call | tf_op jit(solution)/shard_map/swin/pallas_call | solution.py:457
  63.0 1.6 %reshape.3 = bf16[6,6,2,1024]{3,2,1,0:T(2,128)(2,1)} reshape(bf16[72,1024]{1,0:T(8,128)(2,1)} %swin.1) | data formatting | bytes 294912 | tf_op jit(solution)/shard_map/reshape | solution.py:503

commit v5 on v4

--- a/solution.py
+++ b/solution.py
@@ -368,6 +368,11 @@
         return copies
 
     zsend(0)
+    grid_load.wait()
+    for w in range(2):
+        x_ref[144 * w : 144 * w + 144] = grid[:, 6 * w : 6 * w + 6].reshape(144, D)
+    xn[0:ROWS1] = normalize(x_ref[...].astype(F32))
+    zsend(1)
     for ref, (rows, columns, column_of) in zip(
         (p_send, p_own, p_arrive, p_back, p_qown, p_qedge), PERMUTATIONS
     ):
@@ -377,11 +382,6 @@
     bias_ref[0] = jnp.where(column < 72, 0.0, masked_score)
     north = split(row, 6)[1] < 3
     bias_ref[1] = jnp.where(north == (split(column, 6)[1] < 3), 0.0, masked_score)
-    grid_load.wait()
-    for w in range(2):
-        x_ref[144 * w : 144 * w + 144] = grid[:, 6 * w : 6 * w + 6].reshape(144, D)
-    xn[0:ROWS1] = normalize(x_ref[...].astype(F32))
-    zsend(1)
     step_a(0)
     zsend(2)
     step_b(0)

time: 64.8 us -> 64.8 us (level)
  no operation moved by 1% of the time
where the time goes in v5:
time: 64.8 us; the launch traced here: 64.6 us
  Pallas kernels  62.9 us (97%)
  local copies, waits for them, and re-layouts  1.63 us (3%)
    pallas_call x1, Pallas kernels, call(): pl.pallas_call(kernel, out_shape=jax.ShapeDtypeStruct((72, 2 * D), BF16),...  62.9 us
    reshape x1, local copies, waits for them, and re-layouts, body(): return merged.reshape(6, 6, 2, 2 * D)  1.63 us

profile of v5, /device:TPU:1, one launch (start us, length us, event | category | flops | bytes accessed | tf_op | source)
XLA Modules:
  0.0 64.6 jit_solution(3158137666067922053)
XLA Ops:
  0.0 62.9 %swin.1 = bf16[72,1024]{1,0:T(8,128)(2,1)} custom-call(bf16[12,12,2,512]{3,2,1,0:T(2,128)(2,1)} %x_hbm.1, bf16[24,512]{1,0:T(8,128)(2,1)} %bitcast.6, bf16[8,512]{1,0:T(8,128)(2,1)} %bitcast.8, bf16[24,512]{1,0:T(8,128)(2,1)} %bitcast.7, bf16[8,512]{1,0:T(8,128)(2,1)} %bitcast.9, bf16[16,2048]{1,0:T(8,128)(2,1)} %bitcast.5), custom_call_target="tpu_custom_call" | custom-call | tf_op jit(solution)/shard_map/swin/pallas_call | solution.py:457
  63.0 1.6 %reshape.3 = bf16[6,6,2,1024]{3,2,1,0:T(2,128)(2,1)} reshape(bf16[72,1024]{1,0:T(8,128)(2,1)} %swin.1) | data formatting | bytes 294912 | tf_op jit(solution)/shard_map/reshape | solution.py:503
